TPU v7x, 128 devices: a whole 4x4x4 slice. The times are simulated.
128 devices in a mesh: row: 4 (over y), col: 32 (over z, x, core).
Axes of the slice: x: 4, y: 4, z: 4, core: 2. Of those that a mesh axis runs over, the one named last changes fastest.
Arguments:
- row_points: bfloat16 [98304, 64], P(('row', 'col')), as said below
- col_points: bfloat16 [32768, 64], P('col'), as said below
- row_logmass: bfloat16 [98304], P(('row', 'col')), may hold values from -4 to 4
- col_logmass: float32 [32768], P('col'), may hold values from -4 to 4
- col_potential: float32 [32768], P('col'), may hold values from -3 to 11
Outputs:
- row_potential: float32 [98304], P('row')
- new_col_potential: float32 [32768], P('col')
Inputs may be any that keep to these rules, and one draw needn't show every extreme that they name: `row_points`: latent coordinates. `col_points`: latent coordinates.
All inputs are finite; a program needn't handle non-finite values.
Results may differ from a plain program's by a relative error of at most 0.0008.
Values may be sent and summed in bfloat16 or wider, within the bound.
No kernel may reach another device: no remote copies, remote signals or barrier semaphores. Data moves between devices by JAX's collectives and lax.ppermute only.
A program may use at most 64 MiB of HBM per device.

v0:
```python
import jax
import jax.numpy as jnp
from jax import lax
from jax.sharding import PartitionSpec as P

epsilon = 0.05
tile_rows = 1024


def tile_cost(points_in, columns, col_norm):
    widened = points_in.astype(jnp.float32)
    row_norm = jnp.sum(widened * widened, axis=1)
    cross = lax.dot_general(
        points_in, columns, (((1,), (1,)), ((), ())), preferred_element_type=jnp.float32
    )
    return row_norm[:, None] + col_norm[None, :] - 2.0 * cross


def merge_columns(highest, totals):
    global_peak = lax.pmax(highest.astype(jnp.bfloat16), "col").astype(highest.dtype)
    totals = lax.psum((totals * jnp.exp(highest - global_peak)).astype(jnp.bfloat16), "col").astype(
        jnp.float32
    )
    highest = global_peak
    return -epsilon * (highest + jnp.log(totals))


def merge_rows(highest, totals):
    global_peak = lax.pmax(highest, "row")
    totals = lax.psum(totals * jnp.exp(highest - global_peak), "row")
    highest = global_peak
    return -epsilon * (highest + jnp.log(totals))


def body(row_points, col_points, row_logmass, col_logmass, col_potential):
    col_wide = col_points.astype(jnp.float32)
    col_norm = jnp.sum(col_wide * col_wide, axis=1)

    def forward_tile(points_in):
        sq_cost = tile_cost(points_in, col_points, col_norm)
        scores = (col_potential[None, :] - sq_cost) / epsilon + col_logmass[None, :]
        highest = jnp.max(scores, axis=1)
        totals = jnp.sum(jnp.exp(scores - highest[:, None]), axis=1)
        return (highest, totals)

    def backward_tile(running, points_in, logmass, potential_in):
        sq_cost = tile_cost(points_in, col_points, col_norm)
        scores = (potential_in[:, None] - sq_cost) / epsilon + logmass.astype(jnp.float32)[:, None]
        new_peak = jnp.maximum(running[0], jnp.max(scores, axis=0))
        new_total = running[1] * jnp.exp(running[0] - new_peak) + jnp.sum(
            jnp.exp(scores - new_peak[None, :]), axis=0
        )
        return (new_peak, new_total)

    start_state = (
        jnp.full((col_points.shape[0],), -jnp.inf, jnp.float32),
        jnp.zeros((col_points.shape[0],), jnp.float32),
    )
    block_points, block_mass = (
        lax.all_gather(row_points, "col", axis=0, tiled=True),
        lax.all_gather(row_logmass, "col", axis=0, tiled=True),
    )
    count_rows = block_points.shape[0]
    stacked = block_points.reshape(count_rows // tile_rows, tile_rows, block_points.shape[1])
    highest, totals = lax.map(forward_tile, stacked)
    highest, totals = (highest.reshape(count_rows), totals.reshape(count_rows))
    row_potential = merge_columns(highest, totals)
    count_rows = block_points.shape[0]
    splits = count_rows // tile_rows

    def step_tile(state, triple):
        return (backward_tile(state, triple[0], triple[1], triple[2]), None)

    result, unused = lax.scan(
        step_tile,
        start_state,
        (
            block_points.reshape(splits, tile_rows, block_points.shape[1]),
            block_mass.reshape(splits, tile_rows),
            row_potential.reshape(splits, tile_rows),
        ),
    )
    column_peak, column_total = result
    new_col_potential = merge_rows(column_peak, column_total)
    return (row_potential, new_col_potential)


def solution(mesh):
    return jax.shard_map(
        body,
        mesh=mesh,
        in_specs=(P(("row", "col"), None), P("col", None), P(("row", "col")), P("col"), P("col")),
        out_specs=(P("row"), P("col")),
        check_vma=False,
    )
```

profile of v0, /device:TPU:0, one launch (start us, length us, event | category | flops | bytes accessed | tf_op | source)
XLA Modules:
  0.0 594.2 jit_solution(10335809878719593074)
XLA Ops:
  8.6 25.8 %all-gather = bf16[32,1,768]{2,1,0:T(2,128)(2,1)S(1)} all-gather(bf16[1,1,768]{2,1,0:T(2,128)(2,1)S(1)} %reshape.43), channel_id=1, replica_groups=mesh['row'=4,'col'=32] {'col'}, dimensions={0}, use_global_device_ids=true | all-gather | bytes 50688 | tf_op jit(solution)/shard_map/all_gather | solution.py:61
  35.8 22.4 %all-gather.3.cloned.1.call-done = bf16[24576,64]{0,1:T(8,128)(2,1)} async-done(((bf16[768,64]{0,1:T(8,128)(2,1)}), bf16[24576,64]{0,1:T(8,128)(2,1)}) %all-gather.3.cloned.1.call-update) | async-done | bytes 3145744 | tf_op jit(solution)/shard_map/all_gather | solution.py:60
  58.2 6.6 %copy.9 = bf16[24576,64]{1,0:T(8,128)(2,1)} copy(bf16[24576,64]{0,1:T(8,128)(2,1)} %all-gather.3.cloned.1.call-done) | data formatting | bytes 6291456 | tf_op jit(solution)/shard_map/all_gather | solution.py:60
  64.8 127.7 %while.25 = (s32[]{:T(128)}, f32[24,1024]{1,0:T(8,128)S(1)}, f32[24,1024]{1,0:T(8,128)S(1)}, f32[1024]{0:T(1024)S(1)}, bf16[24,1024,64]{2,1,0:T(8,128)(2,1)}, /*...) while((s32[]{:T(128)}, f32[24,1024]{1,0:T(8,128)S(1)}, ...), condition=%wide.region_5.6_spmd, body=%wide.region_1.5_spmd.sunk | while | flops 150139904 | bytes 8978557 | solution.py:65
  66.0 2.3 fusion.23
  71.3 2.3 fusion.23
  76.7 2.3 fusion.23
  82.0 2.3 fusion.23
  87.3 2.3 fusion.23
  92.6 2.3 fusion.23
  98.0 2.3 fusion.23
  103.3 2.3 fusion.23
  108.6 2.3 fusion.23
  113.9 2.3 fusion.23
  119.2 2.3 fusion.23
  124.6 2.3 fusion.23
  129.9 2.3 fusion.23
  135.2 2.3 fusion.23
  140.5 2.3 fusion.23
  145.9 2.3 fusion.23
  151.2 2.3 fusion.23
  156.5 2.3 fusion.23
  161.8 2.3 fusion.23
  167.1 2.3 fusion.23
  172.5 2.3 fusion.23
  177.8 2.3 fusion.23
  183.1 2.3 fusion.23
  188.4 2.3 fusion.23
  192.7 126.3 %pmax.14 = bf16[24576]{0:T(1024)(128)(2,1)S(1)} all-reduce(bf16[24576]{0:T(1024)(128)(2,1)S(1)} %convert_element_type.32), channel_id=1, replica_groups=mesh['row'=4,'col'=32] {'col'}, use_global_device_ids=true, to_apply=%region_6.7 | all-reduce | flops 24576 | bytes 98304 | tf_op jit(solution)/shard_map/pmax | solution.py:20
  319.0 123.8 %psum.14 = bf16[24576]{0:T(1024)(128)(2,1)S(1)} all-reduce(bf16[24576]{0:T(1024)(128)(2,1)S(1)} %fusion.13), channel_id=1, replica_groups=mesh['row'=4,'col'=32] {'col'}, use_global_device_ids=true, to_apply=%region_7.8 | all-reduce | flops 24576 | bytes 98304 | tf_op jit(solution)/shard_map/psum | solution.py:21
  443.5 125.2 %while.26 = (s32[]{:T(128)}, f32[1024]{0:T(1024)S(1)}, f32[1024]{0:T(1024)S(1)}, f32[24,1024]{1,0:T(8,128)S(1)}, bf16[24,1024,64]{2,1,0:T(8,128)(2,1)}, /*index=...) while((s32[]{:T(128)}, f32[1024]{0:T(1024)S(1)}, ...), condition=%wide.region_12.13_spmd.clone, body=%wide.region_8.12_spmd.clone.sunk | while | flops 150148096 | bytes 9017480 | solution.py:74
  444.7 2.3 fusion.25
  447.1 1.6 exponential_reduce_fusion.5
  450.0 2.3 fusion.25
  452.3 1.6 exponential_reduce_fusion.5
  455.2 2.3 fusion.25
  457.5 1.6 exponential_reduce_fusion.5
  460.4 2.3 fusion.25
  465.6 2.3 fusion.25
  470.8 2.3 fusion.25
  476.0 2.3 fusion.25
  478.4 1.6 exponential_reduce_fusion.5
  481.3 2.3 fusion.25
  486.5 2.3 fusion.25
  491.7 2.3 fusion.25
  496.9 2.3 fusion.25
  502.1 2.3 fusion.25
  507.3 2.3 fusion.25
  512.6 2.3 fusion.25
  514.9 1.6 exponential_reduce_fusion.5
  517.8 2.3 fusion.25
  523.0 2.3 fusion.25
  528.2 2.3 fusion.25
  530.5 1.6 exponential_reduce_fusion.5
  533.4 2.3 fusion.25
  538.6 2.3 fusion.25
  543.9 2.3 fusion.25
  549.1 2.3 fusion.25
  554.3 2.3 fusion.25
  559.5 2.3 fusion.25
  564.7 2.3 fusion.25
  567.1 1.6 exponential_reduce_fusion.5
  568.7 10.3 %pmax.15 = f32[1024]{0:T(1024)S(1)} all-reduce(f32[1024]{0:T(1024)S(1)} %get-tuple-element.90), channel_id=1, replica_groups=mesh['row'=4,'col'=32] {'row'}, use_global_device_ids=true, to_apply=%region_13.14 | all-reduce | flops 1024 | bytes 8192 | tf_op jit(solution)/shard_map/pmax | solution.py:29
  579.0 7.7 %psum.15 = f32[1024]{0:T(1024)S(1)} all-reduce(f32[1024]{0:T(1024)S(1)} %exponential_multiply_fusion), channel_id=1, replica_groups=mesh['row'=4,'col'=32] {'row'}, use_global_device_ids=true, to_apply=%region_14.15 | all-reduce | flops 1024 | bytes 8192 | tf_op jit(solution)/shard_map/psum | solution.py:30
  (283 shorter events, 132.2 us)
Async XLA Ops:
  7.2 51.1 %all-gather.3.cloned.1.call-start = ((), (), s32[]{:S(2)}) async-start(), calls=%async_computation | async-start | bytes 3244032 | tf_op jit(solution)/shard_map/all_gather | solution.py:60
  35.7 29.1 %copy-start.1 = (bf16[1024,64]{0,1:T(8,128)(2,1)S(1)}, bf16[1024,64]{0,1:T(8,128)(2,1)}, u32[]{:S(2)}) copy-start(bf16[1024,64]{0,1:T(8,128)(2,1)} %param.10) | copy-start | bytes 393220
  35.8 29.1 %copy-start.2 = (f32[1024]{0:T(1024)S(1)}, f32[1024]{0:T(1024)}, u32[]{:S(2)}) copy-start(f32[1024]{0:T(1024)} %param.13) | copy-start | bytes 12292
  35.8 29.1 %copy-start.3 = (f32[1024]{0:T(1024)S(1)}, f32[1024]{0:T(1024)}, u32[]{:S(2)}) copy-start(f32[1024]{0:T(1024)} %param.12) | copy-start | bytes 12292
  442.9 0.6 copy-start
Sparse Core Ops, SparseCore 0:
  10.4 47.8 all-gather.2
where the time goes:
time: 598 us; the launch traced here: 594 us
  blocking collectives  294 us (49%)
  other arithmetic  136 us (23%)
  matrix products  111 us (19%)
  waiting for transfers between devices  23.1 us (4%)
  between operations  14.2 us (2%)
  local copies, waits for them, and re-layouts  13.7 us (2%)
    pmax x1, blocking collectives, merge_columns(): lax.pmax(highest.astype(jnp.bfloat16), 'col').astype(highest.dtype)  126 us
    psum x1, blocking collectives, merge_columns(): lax.psum((totals * jnp.exp(highest - global_peak)).astype(jnp.bfloat16),...  124 us
    dot_general x48, matrix products, tile_cost(): lax.dot_general(points_in, columns, (((1,), (1,)), ((), ())), preferred_e...  111 us
    reduce_sum x48, other arithmetic, tile_cost(): row_norm = jnp.sum(widened * widened, axis=1)  55.8 us
    reduce_sum x24, other arithmetic, backward_tile(): jnp.sum(jnp.exp(scores - new_peak[None, :]), axis=0)  38.8 us
    reduce_sum x24, other arithmetic, forward_tile(): totals = jnp.sum(jnp.exp(scores - highest[:, None]), axis=1)  38.5 us
    all_gather x1, blocking collectives, body(): lax.all_gather(row_logmass, 'col', axis=0, tiled=True)  25.8 us
    all_gather x1, waiting for transfers between devices, body(): lax.all_gather(row_points, 'col', axis=0, tiled=True)  22.4 us
  transfers between devices with their start and end apart: 1, of which 1 were waited for; matrix products, arithmetic and copies ran while one was open for 0% of the time, Pallas kernels for 0%

commit v1 on v0

v1 whole, which is shorter than its diff:
```python
import jax
import jax.numpy as jnp
from jax import lax
from jax.experimental import pallas as pl
from jax.experimental.pallas import tpu as pltpu
from jax.sharding import Mesh
from jax.sharding import PartitionSpec as P

epsilon = 0.05
dim = 64
rows_own = 768
cols_own = 1024
peers = 8
zs = 4
depth = 80
ln2 = 0.6931471805599453
kappa = 40.0 / ln2
margin = 80.0
chunk = 256
finite_max = 3.0e38


def split3(v):
    first = v.astype(jnp.bfloat16)
    rest = v - first.astype(jnp.float32)
    second = rest.astype(jnp.bfloat16)
    third = (rest - second.astype(jnp.float32)).astype(jnp.bfloat16)
    return first, second, third


def place(rows, width):
    index = lax.broadcasted_iota(jnp.int32, (16, width), 0)
    block = jnp.zeros((16, width), jnp.float32)
    for at, row in rows:
        block = jnp.where(index == at, jnp.broadcast_to(row, (16, width)), block)
    return block.astype(jnp.bfloat16)


def prepare_kernel(x, mass, y, pot, logmass, rows_out, cols_out):
    one_r = jnp.ones((1, rows_own), jnp.float32)
    one_c = jnp.ones((1, cols_own), jnp.float32)
    rows_out[0:dim, :] = x[...]
    rows_out[dim:depth, :] = place(
        [(0, one_r), (1, one_r), (2, one_r), (6, mass[...].astype(jnp.float32))], rows_own
    )
    yw = y[...].astype(jnp.float32)
    norm = jnp.sum(yw * yw, axis=0, keepdims=True)
    c = 0.5 * (pot[...] - norm) + (0.5 * epsilon) * logmass[...]
    c1, c2, c3 = split3(c)
    cols_out[0:dim, :] = y[...]
    cols_out[dim:depth, :] = place(
        [(0, c1.astype(jnp.float32)), (1, c2.astype(jnp.float32)), (2, c3.astype(jnp.float32)),
         (3, one_c), (4, one_c), (5, one_c)], cols_own
    )


def score(left, right):
    return lax.dot_general(
        left, right, (((1,), (0,)), ((), ())), preferred_element_type=jnp.float32
    )


def forward_kernel(rows, cols, out, ys):
    width = rows_own
    total_cols = zs * cols_own
    for q in range(zs):
        for t in range(cols_own // 128):
            tile = cols[q, :, t * 128:(t + 1) * 128]
            tile = jnp.concatenate([tile, jnp.zeros((128 - depth, 128), jnp.bfloat16)], axis=0)
            ys[pl.ds(q * cols_own + t * 128, 128), :] = tile.T

    def block(b, carry):
        right = rows[b]
        sample = score(ys[0:128, 0:depth], right)
        shift = kappa * jnp.max(sample, axis=0, keepdims=True) + margin
        acc = jnp.zeros((8, width), jnp.float32)
        for u in range(total_cols // chunk):
            s = score(ys[u * chunk:(u + 1) * chunk, 0:depth], right)
            p = jnp.exp2(s * kappa - shift)
            acc = acc + jnp.sum(p.reshape(chunk // 8, 8, width), axis=0)
        out[pl.ds(b, 1), :] = shift + jnp.log2(jnp.sum(acc, axis=0, keepdims=True))
        return carry

    lax.fori_loop(0, peers, block, 0)

    @pl.when(jnp.logical_not(jnp.max(out[...]) < finite_max))
    def _():
        def exact(b, carry):
            right = rows[b]

            def peak_step(u, peak):
                s = score(ys[pl.ds(pl.multiple_of(u * chunk, chunk), chunk), 0:depth], right)
                return jnp.maximum(peak, jnp.max(s, axis=0, keepdims=True))

            peak = lax.fori_loop(
                0, total_cols // chunk, peak_step, jnp.full((1, width), -finite_max, jnp.float32)
            )

            def sum_step(u, acc):
                s = score(ys[pl.ds(pl.multiple_of(u * chunk, chunk), chunk), 0:depth], right)
                return acc + jnp.sum(jnp.exp2((s - peak) * kappa), axis=0, keepdims=True)

            total = lax.fori_loop(
                0, total_cols // chunk, sum_step, jnp.zeros((1, width), jnp.float32)
            )
            out[pl.ds(b, 1), :] = kappa * peak + jnp.log2(total)
            return carry

        lax.fori_loop(0, peers, exact, 0)


def merge_kernel(parts, rows, potential, ready):
    peak = parts[0]
    for i in range(1, peers):
        peak = jnp.maximum(peak, parts[i])
    total = jnp.exp2(parts[0] - peak)
    for i in range(1, peers):
        total = total + jnp.exp2(parts[i] - peak)
    merged = peak + jnp.log2(total)
    for b in range(peers):
        xw = rows[b, 0:dim, :].astype(jnp.float32)
        norm = jnp.sum(xw * xw, axis=0, keepdims=True)
        mine = merged[b:b + 1, :]
        potential[b:b + 1, :] = norm - (epsilon * ln2) * mine
        extras = rows[b, dim:depth, :]
        mass = extras.astype(jnp.float32)[6:7, :]
        r1, r2, r3 = split3(mass * (0.5 * epsilon) - mine * (1.0 / kappa))
        one = jnp.ones((1, rows_own), jnp.float32)
        ready[b, 0:dim, :] = rows[b, 0:dim, :]
        ready[b, dim:depth, :] = place(
            [(0, one), (1, one), (2, one), (3, r1.astype(jnp.float32)),
             (4, r2.astype(jnp.float32)), (5, r3.astype(jnp.float32))], rows_own
        )


def backward_kernel(rows, ys, out, acc, shift):
    total_cols = zs * cols_own
    steps = total_cols // chunk
    for u in range(steps):
        at = slice(u * chunk, (u + 1) * chunk)
        s = score(ys[at, 0:depth], rows[0, :, 0:256])
        top = jnp.max(jnp.maximum(s[:, 0:128], s[:, 128:256]), axis=1, keepdims=True)
        shift[at, :] = jnp.broadcast_to(top * kappa + margin, (chunk, 128))
        acc[at, :] = jnp.zeros((chunk, 128), jnp.float32)

    def block(b, carry):
        right = rows[b]
        for u in range(steps):
            at = slice(u * chunk, (u + 1) * chunk)
            s = score(ys[at, 0:depth], right)
            base = shift[at, :]
            run = acc[at, :]
            for t in range(rows_own // 128):
                run = run + jnp.exp2(s[:, t * 128:(t + 1) * 128] * kappa - base)
            acc[at, :] = run
        return carry

    lax.fori_loop(0, peers, block, 0)

    def finish(u, worst):
        at = pl.ds(pl.multiple_of(u * 128, 128), 128)
        total = jnp.sum(acc[at, :], axis=1, keepdims=True)
        logs = shift[at, :] + jnp.log2(jnp.broadcast_to(total, (128, 128)))
        line = logs.T[0:1, :]
        out[pl.ds(u, 1), :] = line
        return jnp.maximum(worst, line)

    worst = lax.fori_loop(
        0, total_cols // 128, finish, jnp.full((1, 128), -finite_max, jnp.float32)
    )

    @pl.when(jnp.logical_not(jnp.max(worst) < finite_max))
    def _():
        def exact(u, carry):
            left = ys[pl.ds(pl.multiple_of(u * 128, 128), 128), 0:depth]

            def peak_step(b, peak):
                s = score(left, rows[b])
                return jnp.maximum(peak, jnp.max(s, axis=1, keepdims=True))

            peak = lax.fori_loop(
                0, peers, peak_step, jnp.full((128, 1), -finite_max, jnp.float32)
            )

            def sum_step(b, total):
                s = score(left, rows[b])
                return total + jnp.sum(jnp.exp2((s - peak) * kappa), axis=1, keepdims=True)

            total = lax.fori_loop(0, peers, sum_step, jnp.zeros((128, 1), jnp.float32))
            logs = jnp.broadcast_to(peak * kappa + jnp.log2(total), (128, 128))
            out[pl.ds(u, 1), :] = logs.T[0:1, :]
            return carry

        lax.fori_loop(0, total_cols // 128, exact, 0)


def final_kernel(parts, pot, logmass, out):
    values = parts[...]
    peak = jnp.max(values, axis=0, keepdims=True)
    total = jnp.sum(jnp.exp2(values - peak), axis=0, keepdims=True)
    merged = peak + jnp.log2(total)
    out[...] = pot[...] + epsilon * logmass[...] - (epsilon * ln2) * merged


def params(mib):
    return pltpu.CompilerParams(vmem_limit_bytes=mib << 20)


def to_all(value, axes, count):
    return lax.all_to_all(jnp.broadcast_to(value[None], (count,) + value.shape), axes, 0, 0)


def body(row_points, col_points, row_logmass, col_logmass, col_potential):
    total_cols = zs * cols_own
    pot = col_potential.reshape(1, cols_own)
    mass_c = col_logmass.reshape(1, cols_own)
    rows_msg, cols_msg = pl.pallas_call(
        prepare_kernel,
        out_shape=(
            jax.ShapeDtypeStruct((depth, rows_own), jnp.bfloat16),
            jax.ShapeDtypeStruct((depth, cols_own), jnp.bfloat16),
        ),
        compiler_params=params(16),
        name="prepare",
    )(row_points.T, row_logmass.reshape(1, rows_own), col_points.T, pot, mass_c)
    rows = to_all(rows_msg, ("x", "k"), peers)
    cols = to_all(cols_msg, "z", zs)
    partial_rows, ys = pl.pallas_call(
        forward_kernel,
        out_shape=(
            jax.ShapeDtypeStruct((peers, rows_own), jnp.float32),
            jax.ShapeDtypeStruct((total_cols, 128), jnp.bfloat16),
        ),
        compiler_params=params(40),
        name="forward",
    )(rows, cols)
    parts = to_all(partial_rows, ("x", "k"), peers)
    potential, ready = pl.pallas_call(
        merge_kernel,
        out_shape=(
            jax.ShapeDtypeStruct((peers, rows_own), jnp.float32),
            jax.ShapeDtypeStruct((peers, depth, rows_own), jnp.bfloat16),
        ),
        compiler_params=params(16),
        name="merge_rows",
    )(parts, rows)
    row_potential = to_all(potential, "z", zs).reshape(-1)
    partial_cols = pl.pallas_call(
        backward_kernel,
        out_shape=jax.ShapeDtypeStruct((total_cols // 128, 128), jnp.float32),
        scratch_shapes=[
            pltpu.VMEM((total_cols, 128), jnp.float32),
            pltpu.VMEM((total_cols, 128), jnp.float32),
        ],
        compiler_params=params(40),
        name="backward",
    )(ready, ys)
    spread = jnp.tile(partial_cols.reshape(zs, cols_own), (4, 1))
    col_parts = lax.all_to_all(spread, ("y", "z"), 0, 0)
    new_col = pl.pallas_call(
        final_kernel,
        out_shape=jax.ShapeDtypeStruct((1, cols_own), jnp.float32),
        compiler_params=params(16),
        name="merge_cols",
    )(col_parts, pot, mass_c)
    return row_potential, new_col.reshape(cols_own)


def solution(mesh):
    fine = Mesh(mesh.devices.reshape(4, 4, 4, 2), ("y", "z", "x", "k"))
    cols = ("z", "x", "k")
    every = ("y",) + cols
    return jax.shard_map(
        body,
        mesh=fine,
        in_specs=(P(every, None), P(cols, None), P(every), P(cols), P(cols)),
        out_specs=(P("y"), P(cols)),
        check_vma=False,
    )
```

time: 598 us -> 175 us (0.29)
  blocking collectives: 294 us -> 57.4 us
  other arithmetic: 136 us -> 0 us
  matrix products: 111 us -> 0 us
  Pallas kernels: 0 us -> 103 us
  waiting for transfers between devices: 23.1 us -> 5.1 us
  between operations: 14.2 us -> 0.72 us
  local copies, waits for them, and re-layouts: 13.7 us -> 4.75 us
    pmax x2 -> x0, blocking collectives: 137 us -> none  [the longest x1 126 us: merge_columns(): lax.pmax(highest.astype(jnp.bfloat16), 'col').astype(highest.dtype)]
    reduce_sum x97 -> x0, other arithmetic: 134 us -> none  [the longest x48 55.8 us: tile_cost(): row_norm = jnp.sum(widened * widened, axis=1)]
    psum x2 -> x0, blocking collectives: 132 us -> none  [the longest x1 124 us: merge_columns(): lax.psum((totals * jnp.exp(highest - global_peak)).astype(jnp.bfloat16),...]
    dot_general x48 -> x0, matrix products: 111 us -> none  [tile_cost(): lax.dot_general(points_in, columns, (((1,), (1,)), ((), ())), preferred_e...]
    pallas_call x0 -> x5, Pallas kernels: none -> 103 us  [the longest x1 81.8 us: body(): pl.pallas_call(forward_kernel, out_shape=(jax.ShapeDtypeStruct((peers, ro...]
    all_to_all x0 -> x4, blocking collectives: none -> 57.4 us  [the longest x3 44.8 us: to_all(): lax.all_to_all(jnp.broadcast_to(value[None], (count,) + value.shape), axe...]
    all_gather x1 -> x0, blocking collectives: 25.8 us -> none  [body(): lax.all_gather(row_logmass, 'col', axis=0, tiled=True)]
    all_gather x1 -> x0, waiting for transfers between devices: 22.4 us -> none  [body(): lax.all_gather(row_points, 'col', axis=0, tiled=True)]
where the time goes in v1:
time: 175 us; the launch traced here: 174 us
  Pallas kernels  103 us (59%)
  blocking collectives  57.4 us (33%)
  waiting for transfers between devices  5.1 us (3%)
  local copies, waits for them, and re-layouts  4.75 us (3%)
  starting transfers between devices  3.3 us (2%)
    pallas_call x1, Pallas kernels, body(): pl.pallas_call(forward_kernel, out_shape=(jax.ShapeDtypeStruct((peers, ro...  81.8 us
    all_to_all x3, blocking collectives, to_all(): lax.all_to_all(jnp.broadcast_to(value[None], (count,) + value.shape), axe...  44.8 us
    pallas_call x1, Pallas kernels, body(): pl.pallas_call(backward_kernel, out_shape=jax.ShapeDtypeStruct((total_col...  20.4 us
    all_to_all x1, blocking collectives, body(): col_parts = lax.all_to_all(spread, ('y', 'z'), 0, 0)  12.6 us
    all_to_all x1, waiting for transfers between devices, to_all(): lax.all_to_all(jnp.broadcast_to(value[None], (count,) + value.shape), axe...  5.1 us
  transfers between devices with their start and end apart: 1, of which 1 were waited for; matrix products, arithmetic and copies ran while one was open for 0% of the time, Pallas kernels for 0%

profile of v1, /device:TPU:0, one launch (start us, length us, event | category | flops | bytes accessed | tf_op | source)
XLA Modules:
  0.0 174.5 jit_solution(13114285781468599036)
XLA Ops:
  0.6 0.0 copy-start.3
  0.6 0.7 reshape.30.mass
  1.3 0.0 copy-start.2
  1.3 0.0 copy-done.3
  1.3 0.7 copy-done.2
  2.0 0.0 copy-start
  2.0 0.9 copy-done
  2.9 0.0 copy-start.1
  2.9 0.9 copy-done.1
  3.8 0.1 prepare.1
  3.9 0.1 broadcast_in_dim.9
  4.0 16.1 %all_to_all.31.cols = bf16[4,80,1024]{2,1,0:T(8,128)(2,1)S(1)} all-to-all(bf16[4,80,1024]{2,1,0:T(8,128)(2,1)S(1)} %broadcast_in_dim.9), channel_id=1, replica_groups=mesh['y'=4,'z'=4,'x'=4,'k'=2] {'z'}, dimensions={0} | all-to-all | bytes 1310720 | tf_op jit(solution)/shard_map/all_to_all | solution.py:210
  20.0 0.1 broadcast_in_dim.8
  20.1 19.5 %all_to_all.32.rows = bf16[8,80,768]{2,1,0:T(8,128)(2,1)S(1)} all-to-all(bf16[8,80,768]{2,1,0:T(8,128)(2,1)S(1)} %broadcast_in_dim.8), channel_id=1, replica_groups=mesh['y'=4,'z'=4,'x'=4,'k'=2] {'x','k'}, dimensions={0} | all-to-all | bytes 1966080 | tf_op jit(solution)/shard_map/all_to_all | solution.py:210
  39.6 81.8 %forward.1 = (f32[8,768]{1,0:T(8,128)S(1)}, bf16[4096,128]{1,0:T(8,128)(2,1)S(1)}) custom-call(bf16[8,80,768]{2,1,0:T(8,128)(2,1)S(1)} %all_to_all.32.rows, bf16[4,80,1024]{2,1,0:T(8,128)(2,1)S(1)} %all_to_all.31.cols), custom_call_target="tpu_custom_call" | custom-call | tf_op jit(solution)/shard_map/forward/pallas_call | solution.py:228
  121.4 9.2 %all_to_all.33.parts = f32[8,8,768]{2,1,0:T(8,128)S(1)} all-to-all(f32[8,8,768]{2,1,0:T(8,128)S(1)} %broadcast_in_dim.10), channel_id=1, replica_groups=mesh['y'=4,'z'=4,'x'=4,'k'=2] {'x','k'}, dimensions={0} | all-to-all | bytes 393216 | tf_op jit(solution)/shard_map/all_to_all | solution.py:210
  130.6 0.3 merge_rows.1
  130.9 20.4 %backward.1 = f32[32,128]{1,0:T(8,128)S(1)} custom-call(bf16[8,80,768]{2,1,0:T(8,128)(2,1)S(1)} %get-tuple-element.12.rows, bf16[4096,128]{1,0:T(8,128)(2,1)S(1)} %get-tuple-element.13.ys), custom_call_target="tpu_custom_call" | custom-call | tf_op jit(solution)/shard_map/backward/pallas_call | solution.py:248
  151.4 0.1 all_to_all.23
  151.5 12.6 %all_to_all.34 = f32[16,1,1024]{2,1,0:T(1,128)S(1)} all-to-all(f32[16,1,1024]{2,1,0:T(1,128)S(1)} %all_to_all.23), channel_id=1, replica_groups=mesh['y'=4,'z'=4,'x'=4,'k'=2] {'y','z'}, dimensions={0} | all-to-all | bytes 131072 | tf_op jit(solution)/shard_map/all_to_all | solution.py:259
  164.1 0.6 broadcast_in_dim.11
  164.8 3.3 %all-to-all-start.3 = ((f32[4,8,768]{2,1,0:T(8,128)}), f32[4,8,768]{2,1,0:T(8,128)S(1)}, u32[]{:S(2)}, u32[]{:S(2)}) async-start(f32[4,8,768]{2,1,0:T(8,128)} %broadcast_in_dim.11), calls=%async_computation.3 | async-start | bytes 196608 | tf_op jit(solution)/shard_map/all_to_all | solution.py:210
  168.1 0.6 merge_cols.1
  168.7 5.1 %all-to-all-done.3 = f32[4,8,768]{2,1,0:T(8,128)S(1)} async-done(((f32[4,8,768]{2,1,0:T(8,128)}), f32[4,8,768]{2,1,0:T(8,128)S(1)}, u32[]{:S(2)}, u32[]{:S(2)}) %all-to-all-start.3) | async-done | bytes 98336 | tf_op jit(solution)/shard_map/all_to_all | solution.py:210
  173.8 0.6 reshape.33
  (4 shorter events, 0.1 us)
Async XLA Ops:
  0.6 0.7 copy-start.3
  1.3 0.7 copy-start.2
  2.0 0.9 copy-start
  2.9 0.9 copy-start.1
  164.8 9.1 %all-to-all-start.3 = ((f32[4,8,768]{2,1,0:T(8,128)}), f32[4,8,768]{2,1,0:T(8,128)S(1)}, u32[]{:S(2)}, u32[]{:S(2)}) async-start(f32[4,8,768]{2,1,0:T(8,128)} %broadcast_in_dim.11), calls=%async_computation.3 | async-start | bytes 196608 | tf_op jit(solution)/shard_map/all_to_all | solution.py:210
